TPU v7x, 32 devices: a whole 2x2x4 slice. The times are simulated.
32 devices in a mesh: gx: 8 (over z, x), gy: 4 (over y, core).
Axes of the slice: x: 2, y: 2, z: 4, core: 2. Of those that a mesh axis runs over, the one named last changes fastest.
Arguments:
- moving_image: bfloat16 [16, 256, 1024], P(None, 'gx', 'gy'), may hold values from -6 to 6, as said below
- fixed_image: bfloat16 [16, 256, 1024], P(None, 'gx', 'gy'), may hold values from -6 to 6, as said below
- velocity: float32 [3, 16, 256, 1024], P(None, None, 'gx', 'gy'), may hold values from 0 to 1
- offsets: int32 [3, 16, 8], P(None, 'gx', 'gy'), may hold values from -7 to 7, as said below
- tissue: int32 [16, 8], P('gx', 'gy'), may hold values from 0 to 1, as said below
Outputs:
- update: float32 [3, 16, 256, 1024], P(None, None, 'gx', 'gy')
- similarity_loss: float32 [], replicated
Inputs may be any that keep to these rules, and one draw needn't show every extreme that they name: `moving_image`: the images stay within -6 to 6. `fixed_image`: the images stay within -6 to 6. `offsets`: channel 0 lies in -2 to 2, channels 1 and 2 in -7 to 7; each end is taken by some block. 1 marks a block that holds tissue; some blocks hold tissue.
All inputs are finite; a program needn't handle non-finite values.
Results may differ from a plain program's by a relative error of at most 0.0011.
Values may be sent and summed in bfloat16 or wider, within the bound.
A program may use at most 64 MiB of HBM per device.

v0:
```python
import functools
import math

import jax
import jax.numpy as jnp
import numpy as np
from jax import lax
from jax.experimental import pallas as pl
from jax.experimental.pallas import tpu as pltpu
from jax.sharding import PartitionSpec as P

BX = 16
BY = 128
ZREACH = 2
BOX = 4
GAUSS_RADIUS = 7
GAUSS_SIGMA = 3.0
COUNT = 729.0
EPS = 1e-05
STEP_RATE = 16.0
HALO = 16
GHALO = 8
GROUP = 4
F32 = jnp.float32
BF16 = jnp.bfloat16
MESH = pl.DeviceIdType.MESH

DIRS = [(-1, 0), (1, 0), (0, -1), (0, 1), (-1, -1), (-1, 1), (1, -1), (1, 1)]


def dot(a, b):
    return jnp.dot(a, b, preferred_element_type=F32)


def split2(x):
    h = x.astype(BF16)
    return h, (x - h.astype(F32)).astype(BF16)


def split3(x):
    h = x.astype(BF16)
    r = x - h.astype(F32)
    m = r.astype(BF16)
    return h, m, (r - m.astype(F32)).astype(BF16)


def halo_refs(direction, rows, center, left, right):
    dx, dy = direction
    src_rows = {-1: pl.ds(HALO, HALO), 0: pl.ds(HALO, rows), 1: pl.ds(rows, HALO)}[dx]
    dst_rows = {-1: pl.ds(HALO + rows, HALO), 0: pl.ds(HALO, rows), 1: pl.ds(0, HALO)}[dx]
    cols = center.shape[2]
    if dy == 0:
        return center.at[:, src_rows, :], center.at[:, dst_rows, :]
    if dy < 0:
        return center.at[:, src_rows, pl.ds(0, BY)], right.at[:, dst_rows, :]
    return center.at[:, src_rows, pl.ds(cols - BY, BY)], left.at[:, dst_rows, :]


def fused_kernel(
    nx, ny,
    off_ref, tis_ref, mov_ref, fix_ref, vel_hbm,
    gh_ref, gl_ref, acc_ref,
    mC, mL, mR, fC, fL, fR, wC, wL, wR, sC, sL, sR,
    vel, sF, T, Y, A, by_ref, bx_ref,
    vel_sem, send_sem, recv_sem,
):
    depth, rows, cols = mov_ref.shape
    ext = rows + 2 * HALO
    wide = cols + BY
    gx, gy = lax.axis_index("gx"), lax.axis_index("gy")

    def exists(d):
        dx, dy = d
        c = None
        for cond in (
            (gx > 0) if dx < 0 else (gx < nx - 1) if dx > 0 else None,
            (gy > 0) if dy < 0 else (gy < ny - 1) if dy > 0 else None,
        ):
            if cond is not None:
                c = cond if c is None else jnp.logical_and(c, cond)
        return c

    has = [exists(d) for d in DIRS]

    vel_copy = pltpu.make_async_copy(vel_hbm, vel, vel_sem)
    vel_copy.start()

    barrier = pltpu.get_barrier_semaphore()
    for i, (dx, dy) in enumerate(DIRS):
        @pl.when(has[i])
        def _():
            pl.semaphore_signal(barrier, inc=1, device_id=(gx + dx, gy + dy), device_id_type=MESH)

    def clear(center, left, right):
        for i, (dx, dy) in enumerate(DIRS):
            _, dst = halo_refs((-dx, -dy), rows, center, left, right)

            @pl.when(jnp.logical_not(has[i]))
            def _():
                dst[...] = jnp.zeros(dst.shape, dst.dtype)

    mC[:, HALO : HALO + rows, :] = mov_ref[...]
    def line(g, n):
        return 1 + jnp.where(g > 0, 1, 0) + jnp.where(g < n - 1, 1, 0)

    pl.semaphore_wait(barrier, line(gx, nx) * line(gy, ny) - 1)

    def copies(t, center, left, right):
        out = []
        for i, (dx, dy) in enumerate(DIRS):
            src, dst = halo_refs((dx, dy), rows, center, left, right)
            out.append(
                pltpu.make_async_remote_copy(
                    src_ref=src, dst_ref=dst,
                    send_sem=send_sem.at[t, i], recv_sem=recv_sem.at[t, i],
                    device_id=(gx + dx, gy + dy), device_id_type=MESH,
                )
            )
        return out

    def start(cs):
        for i, c in enumerate(cs):
            @pl.when(has[i])
            def _():
                c.start()

    def wait_recv(cs):
        for i, c in enumerate(cs):
            j = DIRS.index((-DIRS[i][0], -DIRS[i][1]))

            @pl.when(has[j])
            def _():
                c.wait_recv()

    def wait_send(cs):
        for i, c in enumerate(cs):
            @pl.when(has[i])
            def _():
                c.wait_send()

    m_copies = copies(0, mC, mL, mR)
    f_copies = copies(1, fC, fL, fR)
    w_copies = copies(2, wC, wL, wR)
    s_copies = copies(3, sC, sL, sR)
    start(m_copies)

    fC[0:depth, HALO : HALO + rows, :] = fix_ref[...]
    for r in range(rows // BX):
        for c in range(cols // BY):
            value = tis_ref[r, c].astype(F32)
            fC[depth, HALO + r * BX : HALO + (r + 1) * BX, c * BY : (c + 1) * BY] = jnp.full(
                (BX, BY), value, F32
            ).astype(BF16)
    start(f_copies)

    clear(mC, mL, mR)
    clear(fC, fL, fR)
    clear(wC, wL, wR)
    clear(sC, sL, sR)

    ki = lax.broadcasted_iota(jnp.int32, (wide, wide), 0)
    ji = lax.broadcasted_iota(jnp.int32, (wide, wide), 1)
    dist = jnp.abs(ki - ji)
    dist = jnp.minimum(dist, wide - dist)
    by_ref[...] = jnp.where(dist <= BOX, 1.0, 0.0).astype(BF16)
    size = GROUP * ext
    ki = lax.broadcasted_iota(jnp.int32, (size, size), 0)
    ji = lax.broadcasted_iota(jnp.int32, (size, size), 1)
    same = (ki // ext) == (ji // ext)
    bx_ref[...] = jnp.where(
        jnp.logical_and(same, jnp.abs(ki - ji) <= BOX), 1.0, 0.0
    ).astype(BF16)
    zpad = ZREACH + 1
    T[0:zpad] = jnp.zeros((zpad,) + T.shape[1:], F32)
    T[depth + zpad :] = jnp.zeros((zpad,) + T.shape[1:], F32)
    for k in range(5):
        Y[k, 0:BOX] = jnp.zeros((BOX, ext, wide), F32)
        Y[k, depth + BOX :] = jnp.zeros((BOX, ext, wide), F32)
    for k in range(3):
        A[k, 0:BOX] = jnp.zeros((BOX, ext, wide), F32)
        A[k, depth + BOX :] = jnp.zeros((BOX, ext, wide), F32)

    def side(left, right):
        lane = lax.broadcasted_iota(jnp.int32, left.shape, left.ndim - 1)
        return jnp.where(lane < BY // 2, right.astype(F32), left.astype(F32))

    def joined(center, left, right):
        s = side(left, right).astype(center.dtype)
        return jnp.concatenate([center, s], axis=-1)

    wait_recv(m_copies)
    vel_copy.wait()

    slab = BX + 2 * HALO
    for br in range(rows // BX):
        for bc in range(cols // BY):
            oz, ox, oy = off_ref[0, br, bc], off_ref[1, br, bc], off_ref[2, br, bc]
            lane = lax.broadcasted_iota(jnp.int32, (wide, 2 * BY), 1)
            target = jnp.where(lane < BY, lane, lane - BY + 1) + bc * BY + oy
            target = jnp.where(target < 0, target + wide, target)
            source = lax.broadcasted_iota(jnp.int32, (wide, 2 * BY), 0)
            shift = jnp.where(source == target, 1.0, 0.0).astype(BF16)
            r0 = br * BX
            i = lax.broadcasted_iota(jnp.int32, (GROUP * 2 * BX, GROUP * slab), 0)
            k = lax.broadcasted_iota(jnp.int32, (GROUP * 2 * BX, GROUP * slab), 1)
            row = (i // (2 * BX)) * slab + HALO + (i % BX) + (i // BX) % 2 + ox
            down = jnp.where(k == row, 1.0, 0.0).astype(BF16)

            def move(g, carry):
                z = pl.multiple_of(g * GROUP, GROUP)
                x = joined(
                    mC[pl.ds(z, GROUP), r0 : r0 + slab, :],
                    mL[pl.ds(z, GROUP), r0 : r0 + slab, :],
                    mR[pl.ds(z, GROUP), r0 : r0 + slab, :],
                )
                t = dot(x.reshape(GROUP * slab, wide), shift).astype(BF16)
                T[pl.ds(z + zpad, GROUP)] = dot(down, t).reshape(GROUP, 2 * BX, 2 * BY)
                return carry

            lax.fori_loop(0, depth // GROUP, move, 0)
            rs = slice(r0, r0 + BX)
            cs = slice(bc * BY, (bc + 1) * BY)
            hs = slice(HALO + r0, HALO + r0 + BX)

            def warp(z, carry):
                f0, f1, f2 = vel[0, z, rs, cs], vel[1, z, rs, cs], vel[2, z, rs, cs]
                planes, slopes_x, slopes_y = [], [], []
                for c in (0, 1):
                    vs, ds = [], []
                    for a in (0, 1):
                        s = T[z + zpad + oz + c, a * BX : (a + 1) * BX, :]
                        low, high = s[:, :BY], s[:, BY:]
                        d = high - low
                        vs.append((1.0 - f2) * low + f2 * high)
                        ds.append(d)
                    planes.append((1.0 - f1) * vs[0] + f1 * vs[1])
                    slopes_x.append(vs[1] - vs[0])
                    slopes_y.append((1.0 - f1) * ds[0] + f1 * ds[1])
                value = (1.0 - f0) * planes[0] + f0 * planes[1]
                wC[z, hs, cs] = value.astype(BF16)
                slopes = (
                    planes[1] - planes[0],
                    (1.0 - f0) * slopes_x[0] + f0 * slopes_x[1],
                    (1.0 - f0) * slopes_y[0] + f0 * slopes_y[1],
                )
                for k in range(3):
                    sF[k, z, rs, cs] = slopes[k]
                    sC[k * depth + z, hs, cs] = slopes[k].astype(BF16)
                return carry

            lax.fori_loop(0, depth, warp, 0)

    start(w_copies)
    start(s_copies)
    wait_recv(f_copies)
    wait_recv(w_copies)

    by = by_ref[...]

    def image(center, left, right, z):
        return joined(center[pl.ds(z, GROUP)], left[pl.ds(z, GROUP)], right[pl.ds(z, GROUP)])

    def stats_y(g, carry):
        z = g * GROUP
        i_low = image(wC, wL, wR, z).reshape(GROUP * ext, wide)
        j_low = image(fC, fL, fR, z).reshape(GROUP * ext, wide)
        i, j = i_low.astype(F32), j_low.astype(F32)
        fields = [(i_low,), (j_low,), split2(i * i), split2(j * j), split2(i * j)]
        for k, parts in enumerate(fields):
            y = dot(parts[0], by)
            for part in parts[1:]:
                y = y + dot(part, by)
            Y[k, pl.ds(z + BOX, GROUP)] = y.reshape(GROUP, ext, wide)
        return carry

    lax.fori_loop(0, depth // GROUP, stats_y, 0)

    def window_z(ref, k, z):
        p = [ref[k, z + t] for t in range(GROUP + 2 * BOX)]
        common = ((p[3] + p[4]) + (p[5] + p[6])) + (p[7] + p[8])
        low, high = p[1] + p[2], p[9] + p[10]
        outs = [
            common + (p[0] + low), common + (low + p[9]),
            common + (p[2] + high), common + (high + p[11]),
        ]
        return jnp.concatenate(outs, axis=0)

    mask = joined(fC[depth], fL[depth], fR[depth]).astype(F32)
    row = lax.broadcasted_iota(jnp.int32, (ext, wide), 0)
    lane = lax.broadcasted_iota(jnp.int32, (ext, wide), 1)
    own = jnp.logical_and(jnp.logical_and(row >= HALO, row < HALO + rows), lane < cols)
    own_mask = jnp.where(own, mask, 0.0)
    acc_ref[...] = jnp.zeros_like(acc_ref)

    def stats(g, carry):
        z = g * GROUP
        sums = []
        for k in range(5):
            h, m, l = split3(window_z(Y, k, z))
            sums.append(dot(bx_ref[...], h) + dot(bx_ref[...], m) + dot(bx_ref[...], l))
        si, sj, sii, sjj, sij = [s.reshape(GROUP, ext, wide) for s in sums]
        cross = sij - si * sj * (1.0 / COUNT)
        var_i = sii - si * si * (1.0 / COUNT)
        var_j = sjj - sj * sj * (1.0 / COUNT)
        q = cross / (var_i * var_j + EPS)
        live = mask[None] > 0.0
        acc_ref[...] += jnp.sum(jnp.where(own_mask[None] > 0.0, cross * q, 0.0), axis=0)
        q = jnp.where(live, q, 0.0)
        p = jnp.where(live, q * q * var_j, 0.0)
        terms = (
            jnp.where(live, (2.0 / COUNT) * (q * sj - p * si), 0.0), p, -2.0 * q,
        )
        for k in range(3):
            h, l = split2(terms[k].reshape(GROUP * ext, wide))
            y = dot(h, by_ref[...]) + dot(l, by_ref[...])
            A[k, pl.ds(z + BOX, GROUP)] = y.reshape(GROUP, ext, wide)
        return carry

    lax.fori_loop(0, depth // GROUP, stats, 0)

    wait_recv(s_copies)
    inner = slice(HALO - GHALO, HALO + rows + GHALO)

    def grads(g, carry):
        z = g * GROUP
        box = []
        for k in range(3):
            h, l = split2(window_z(A, k, z))
            b = dot(bx_ref[...], h) + dot(bx_ref[...], l)
            box.append(b.reshape(GROUP, ext, wide)[:, inner])
        i = image(wC, wL, wR, z).astype(F32)[:, inner]
        j = image(fC, fL, fR, z).astype(F32)[:, inner]
        grad = box[0] + 2.0 * i * box[1] + j * box[2]
        for k in range(3):
            zs = pl.ds(k * depth + z, GROUP)
            c = sC[zs].astype(F32)
            c = jnp.concatenate(
                [c[:, HALO - GHALO : HALO], sF[k, pl.ds(z, GROUP)],
                 c[:, HALO + rows : HALO + rows + GHALO]], axis=1)
            s = side(sL[zs], sR[zs])[:, inner]
            h, l = split2(grad * jnp.concatenate([c, s], axis=-1))
            gh_ref[k, pl.ds(z, GROUP)] = h
            gl_ref[k, pl.ds(z, GROUP)] = l
        return carry

    lax.fori_loop(0, depth // GROUP, grads, 0)
    for cs in (m_copies, f_copies, w_copies, s_copies):
        wait_send(cs)


def smooth_kernel(gh_ref, gl_ref, yh_ref, yl_ref, xh_ref, xl_ref, out_ref):
    _, depth, rows, wide = gh_ref.shape
    h = gh_ref[...].reshape(depth * rows, wide)
    l = gl_ref[...].reshape(depth * rows, wide)
    t = dot(h, yh_ref[...]) + dot(l, yh_ref[...]) + dot(h, yl_ref[...])
    h, l = split2(t)
    o = dot(xh_ref[...], h) + dot(xh_ref[...], l) + dot(xl_ref[...], h)
    out_ref[...] = o.reshape(out_ref.shape)


def gauss():
    taps = np.arange(-GAUSS_RADIUS, GAUSS_RADIUS + 1)
    w = np.exp(-(taps * taps) / (2.0 * GAUSS_SIGMA**2))
    return w / w.sum()


def as_pair(m):
    h = m.astype(jnp.bfloat16)
    return h, (m - h.astype(np.float64)).astype(jnp.bfloat16)


def gauss_y(cols):
    w, wide = gauss(), cols + BY
    m = np.zeros((wide, cols))
    for j in range(cols):
        for t in range(-GAUSS_RADIUS, GAUSS_RADIUS + 1):
            m[(j + t) % wide, j] = w[t + GAUSS_RADIUS]
    return as_pair(m)


def gauss_zx(depth, rows):
    w = gauss()
    mx = np.zeros((rows, rows + 2 * GHALO))
    mz = np.zeros((depth, depth))
    for t in range(-GAUSS_RADIUS, GAUSS_RADIUS + 1):
        for r in range(rows):
            mx[r, r + GHALO + t] = w[t + GAUSS_RADIUS]
        for z in range(depth):
            if 0 <= z + t < depth:
                mz[z, z + t] = w[t + GAUSS_RADIUS]
    return as_pair(-STEP_RATE * np.kron(mz, mx))


def on_device(nx, ny, moving, fixed, velocity, offsets, tissue):
    depth, rows, cols = moving.shape
    ext, wide, gext = rows + 2 * HALO, cols + BY, rows + 2 * GHALO

    def ring(n):
        return [
            pltpu.VMEM((n, ext, cols), BF16),
            pltpu.VMEM((n, ext, BY), BF16),
            pltpu.VMEM((n, ext, BY), BF16),
        ]

    vmem = pl.BlockSpec(memory_space=pltpu.VMEM)
    smem = pl.BlockSpec(memory_space=pltpu.SMEM)
    gshape = jax.ShapeDtypeStruct((3, depth, gext, wide), BF16)
    gh, gl, acc = pl.pallas_call(
        functools.partial(fused_kernel, nx, ny),
        out_shape=(gshape, gshape, jax.ShapeDtypeStruct((ext, wide), F32)),
        in_specs=[smem, smem, vmem, vmem, pl.BlockSpec(memory_space=pl.ANY)],
        out_specs=(vmem, vmem, vmem),
        scratch_shapes=[
            *ring(depth), *ring(depth + 1), *ring(depth), *ring(3 * depth),
            pltpu.VMEM(velocity.shape, F32),
            pltpu.VMEM((3, depth, rows, cols), F32),
            pltpu.VMEM((depth + 2 * (ZREACH + 1), 2 * BX, 2 * BY), F32),
            pltpu.VMEM((5, depth + 2 * BOX, ext, wide), F32),
            pltpu.VMEM((3, depth + 2 * BOX, ext, wide), F32),
            pltpu.VMEM((wide, wide), BF16),
            pltpu.VMEM((GROUP * ext, GROUP * ext), BF16),
            pltpu.SemaphoreType.DMA,
            pltpu.SemaphoreType.DMA((4, 8)),
            pltpu.SemaphoreType.DMA((4, 8)),
        ],
        compiler_params=pltpu.CompilerParams(
            collective_id=0, has_side_effects=True, vmem_limit_bytes=56 * 2**20
        ),
    )(offsets, tissue, moving, fixed, velocity)
    totals = lax.psum(
        jnp.stack([jnp.sum(acc), jnp.sum(tissue).astype(F32)]), ("gx", "gy")
    )
    loss = -totals[0] / (totals[1] * float(BX * BY * depth))

    yh, yl = gauss_y(cols)
    xh, xl = gauss_zx(depth, rows)
    gspec = pl.BlockSpec((1, depth, gext, wide), lambda k: (k, 0, 0, 0))
    whole = lambda a: pl.BlockSpec(a.shape, lambda k: (0, 0))
    update = pl.pallas_call(
        smooth_kernel,
        grid=(3,),
        out_shape=jax.ShapeDtypeStruct((3, depth, rows, cols), F32),
        in_specs=[gspec, gspec, whole(yh), whole(yl), whole(xh), whole(xl)],
        out_specs=pl.BlockSpec((1, depth, rows, cols), lambda k: (k, 0, 0, 0)),
        compiler_params=pltpu.CompilerParams(vmem_limit_bytes=48 * 2**20),
    )(gh, gl, jnp.asarray(yh), jnp.asarray(yl), jnp.asarray(xh), jnp.asarray(xl))
    return update, loss


def solution(mesh):
    in_specs = (
        P(None, "gx", "gy"),
        P(None, "gx", "gy"),
        P(None, None, "gx", "gy"),
        P(None, "gx", "gy"),
        P("gx", "gy"),
    )
    out_specs = (P(None, None, "gx", "gy"), P())
    return jax.shard_map(
        functools.partial(on_device, mesh.shape["gx"], mesh.shape["gy"]),
        mesh=mesh, in_specs=in_specs, out_specs=out_specs, check_vma=False,
    )
```

profile of v0, /device:TPU:0, one launch (start us, length us, event | category | flops | bytes accessed | tf_op | source)
XLA Modules:
  0.0 137.2 jit_solution(5369471904872106477)
XLA Ops:
  0.6 0.0 copy-start.2
  0.6 0.0 copy-start.3
  0.7 0.0 copy-start.4
  0.7 0.0 copy-start.5
  0.7 1.5 %reduce_sum.19 = s32[]{:T(128)} reduce(s32[2,2]{1,0:T(2,128)} %tis_ref.1, s32[]{:T(128)} %constant.6.clone.1), dimensions={0,1}, to_apply=%region_1.0 | reduce | flops 3 | bytes 24 | tf_op jit(solution)/shard_map/reduce_sum | solution.py:431
  2.8 1.3 copy.11.off_ref
  4.1 62.5 %shard_map.104 = (bf16[3,16,48,384]{3,2,1,0:T(8,128)(2,1)}, bf16[3,16,48,384]{3,2,1,0:T(8,128)(2,1)}, f32[64,384]{1,0:T(8,128)}) custom-call(s32[3,2,2]{2,1,0:T(2,128)} %copy.11.off_ref, s32[2,2]{1,0:T(2,128)} %tis_ref.1, bf16[16,32,256]{2,1,0:T(8,128)(2,1)} %mov_ref.1, bf16[16,32,256]{2,1,0:T(8,128)(2,1)} %fix_ref.1, f32[3,16,32,256]{3,2,1,0:T(8,128)} %vel_hbm.1), custom_call_target="tpu_custom_call" | custom-call | tf_op jit(solution)/shard_map/pallas_call | solution.py:408
  66.6 1.5 %reduce_sum.18 = f32[]{:T(128)} reduce(f32[64,384]{1,0:T(8,128)} %get-tuple-element.7, f32[]{:T(128)} %constant.5.clone.1), dimensions={0,1}, to_apply=%region_0.0 | reduce | flops 24575 | bytes 98312 | tf_op jit(solution)/shard_map/reduce_sum | solution.py:431
  68.1 0.7 pad_maximum_fusion
  68.8 53.8 %psum.7 = f32[2]{0:T(128)S(1)} all-reduce(f32[2]{0:T(128)S(1)} %pad_maximum_fusion), channel_id=1, replica_groups=mesh['gx'=8,'gy'=4] {'gx','gy'}, use_global_device_ids=true, to_apply=%region_2.0 | all-reduce | flops 2 | bytes 16 | tf_op jit(solution)/shard_map/psum | solution.py:430
  122.6 0.0 copy-done.2
  122.6 0.0 copy-done.3
  122.6 0.0 copy-done.4
  122.6 0.0 copy-done.5
  122.6 0.0 copy-start
  122.6 1.5 %copy-done = bf16[3,16,48,384]{3,2,1,0:T(8,128)(2,1)S(1)} copy-done((bf16[3,16,48,384]{3,2,1,0:T(8,128)(2,1)S(1)}, bf16[3,16,48,384]{3,2,1,0:T(8,128)(2,1)}, u32[]{:S(2)}) %copy-start) | copy-done | bytes 1769496
  124.1 0.0 copy-start.1
  124.1 1.5 %copy-done.1 = bf16[3,16,48,384]{3,2,1,0:T(8,128)(2,1)S(1)} copy-done((bf16[3,16,48,384]{3,2,1,0:T(8,128)(2,1)S(1)}, bf16[3,16,48,384]{3,2,1,0:T(8,128)(2,1)}, u32[]{:S(2)}) %copy-start.1) | copy-done | bytes 1769496
  125.6 8.5 %shard_map.105 = f32[3,16,32,256]{3,2,1,0:T(8,128)} custom-call(bf16[3,16,48,384]{3,2,1,0:T(8,128)(2,1)S(1)} %copy-done, bf16[3,16,48,384]{3,2,1,0:T(8,128)(2,1)S(1)} %copy-done.1, bf16[384,256]{1,0:T(8,128)(2,1)S(1)} %copy-done.5, bf16[384,256]{1,0:T(8,128)(2,1)S(1)} %copy-done.4, bf16[512,768]{1,0:T(8,128)(2,1)S(1)} %copy-done.3, ...), custom_call_target="tpu_custom_call" | custom-call | tf_op jit(solution)/shard_map/pallas_call | solution.py:439
  134.1 0.6 fusion
Async XLA Ops:
  0.6 122.0 %copy-start.2 = (bf16[512,768]{1,0:T(8,128)(2,1)S(1)}, bf16[512,768]{1,0:T(8,128)(2,1)}, u32[]{:S(2)}) copy-start(bf16[512,768]{1,0:T(8,128)(2,1)} %constant.18.clone.xl_ref) | copy-start | bytes 2359300
  0.6 122.0 %copy-start.3 = (bf16[512,768]{1,0:T(8,128)(2,1)S(1)}, bf16[512,768]{1,0:T(8,128)(2,1)}, u32[]{:S(2)}) copy-start(bf16[512,768]{1,0:T(8,128)(2,1)} %constant.17.clone.xh_ref) | copy-start | bytes 2359300
  0.7 122.0 %copy-start.4 = (bf16[384,256]{1,0:T(8,128)(2,1)S(1)}, bf16[384,256]{1,0:T(8,128)(2,1)}, u32[]{:S(2)}) copy-start(bf16[384,256]{1,0:T(8,128)(2,1)} %constant.16.clone.yl_ref) | copy-start | bytes 589828
  0.7 121.9 %copy-start.5 = (bf16[384,256]{1,0:T(8,128)(2,1)S(1)}, bf16[384,256]{1,0:T(8,128)(2,1)}, u32[]{:S(2)}) copy-start(bf16[384,256]{1,0:T(8,128)(2,1)} %constant.15.clone.yh_ref) | copy-start | bytes 589828
  122.6 1.5 %copy-start = (bf16[3,16,48,384]{3,2,1,0:T(8,128)(2,1)S(1)}, bf16[3,16,48,384]{3,2,1,0:T(8,128)(2,1)}, u32[]{:S(2)}) copy-start(bf16[3,16,48,384]{3,2,1,0:T(8,128)(2,1)} %get-tuple-element.5.gh_ref) | copy-start | bytes 5308420
  124.1 1.5 %copy-start.1 = (bf16[3,16,48,384]{3,2,1,0:T(8,128)(2,1)S(1)}, bf16[3,16,48,384]{3,2,1,0:T(8,128)(2,1)}, u32[]{:S(2)}) copy-start(bf16[3,16,48,384]{3,2,1,0:T(8,128)(2,1)} %get-tuple-element.6.gl_ref) | copy-start | bytes 5308420
where the time goes:
time: 138 us; the launch traced here: 137 us
  Pallas kernels  70.9 us (51%)
  blocking collectives  53.8 us (39%)
  local copies, waits for them, and re-layouts  4.91 us (4%)
  between operations  3.85 us (3%)
  other arithmetic  3.69 us (3%)
    pallas_call x1, Pallas kernels, on_device(): pl.pallas_call(functools.partial(fused_kernel, nx, ny), out_shape=(gshape...  62.5 us
    psum x1, blocking collectives, on_device(): lax.psum(jnp.stack([jnp.sum(acc), jnp.sum(tissue).astype(F32)]), ('gx', '...  53.8 us
    pallas_call x1, Pallas kernels, on_device(): pl.pallas_call(smooth_kernel, grid=(3,), out_shape=jax.ShapeDtypeStruct((...  8.48 us
    unnamed x13, local copies, waits for them, and re-layouts  4.32 us

commit v1 on v0

--- a/solution.py
+++ b/solution.py
@@ -58,11 +58,12 @@
 
 def fused_kernel(
     nx, ny,
-    off_ref, tis_ref, mov_ref, fix_ref, vel_hbm,
-    gh_ref, gl_ref, acc_ref,
+    off_ref, tis_ref, mov_ref, fix_ref, vel_hbm, yh_hbm, yl_hbm, xh_hbm, xl_hbm,
+    out_hbm, loss_ref,
     mC, mL, mR, fC, fL, fR, wC, wL, wR, sC, sL, sR,
     vel, sF, T, Y, A, by_ref, bx_ref,
-    vel_sem, send_sem, recv_sem,
+    gh_ref, gl_ref, out, yh, yl, xh, xl, acc_ref, part, by_y, by_x,
+    vel_sem, const_sem, out_sem, send_sem, recv_sem, ysend_sem, yrecv_sem, xsend_sem, xrecv_sem,
 ):
     depth, rows, cols = mov_ref.shape
     ext = rows + 2 * HALO
@@ -84,6 +85,12 @@
 
     vel_copy = pltpu.make_async_copy(vel_hbm, vel, vel_sem)
     vel_copy.start()
+    const_copies = [
+        pltpu.make_async_copy(a, b, const_sem.at[i])
+        for i, (a, b) in enumerate(((yh_hbm, yh), (yl_hbm, yl), (xh_hbm, xh), (xl_hbm, xl)))
+    ]
+    for c in const_copies:
+        c.start()
 
     barrier = pltpu.get_barrier_semaphore()
     for i, (dx, dy) in enumerate(DIRS):
@@ -91,6 +98,15 @@
         def _():
             pl.semaphore_signal(barrier, inc=1, device_id=(gx + dx, gy + dy), device_id_type=MESH)
 
+    for d in range(1, ny):
+        pl.semaphore_signal(
+            barrier, inc=1, device_id=(gx, lax.rem(gy + d, ny)), device_id_type=MESH
+        )
+    for d in range(1, nx):
+        pl.semaphore_signal(
+            barrier, inc=1, device_id=(lax.rem(gx + d, nx), gy), device_id_type=MESH
+        )
+
     def clear(center, left, right):
         for i, (dx, dy) in enumerate(DIRS):
             _, dst = halo_refs((-dx, -dy), rows, center, left, right)
@@ -103,7 +119,7 @@
     def line(g, n):
         return 1 + jnp.where(g > 0, 1, 0) + jnp.where(g < n - 1, 1, 0)
 
-    pl.semaphore_wait(barrier, line(gx, nx) * line(gy, ny) - 1)
+    pl.semaphore_wait(barrier, line(gx, nx) * line(gy, ny) - 1 + (ny - 1) + (nx - 1))
 
     def copies(t, center, left, right):
         out = []
@@ -318,6 +334,35 @@
 
     lax.fori_loop(0, depth // GROUP, stats, 0)
 
+    def folded(x):
+        x = sum(x[r : r + 8] for r in range(0, ext, 8))
+        return sum(x[:, c : c + BY] for c in range(0, wide, BY))
+
+    blocks = 0
+    for r in range(rows // BX):
+        for c in range(cols // BY):
+            blocks = blocks + tis_ref[r, c]
+    part[0, 0:8] = folded(acc_ref[...])
+    part[0, 8:16] = jnp.full((8, BY), blocks.astype(F32), F32)
+
+    def spread(n, axis_of, src, dst, ssem, rsem):
+        return [
+            pltpu.make_async_remote_copy(
+                src_ref=src, dst_ref=dst.at[d], send_sem=ssem.at[d], recv_sem=rsem.at[d],
+                device_id=axis_of(d), device_id_type=MESH,
+            )
+            for d in range(1, n)
+        ]
+
+    y_copies = spread(
+        ny, lambda d: (gx, lax.rem(gy + d, ny)), part.at[0], by_y, ysend_sem, yrecv_sem
+    )
+    x_copies = spread(
+        nx, lambda d: (lax.rem(gx + d, nx), gy), part.at[1], by_x, xsend_sem, xrecv_sem
+    )
+    for c in y_copies:
+        c.start()
+
     wait_recv(s_copies)
     inner = slice(HALO - GHALO, HALO + rows + GHALO)
 
@@ -344,18 +389,43 @@
         return carry
 
     lax.fori_loop(0, depth // GROUP, grads, 0)
+
+    for c in y_copies:
+        c.wait()
+    total = part[0]
+    for d in range(1, ny):
+        total = total + by_y[d]
+    part[1] = total
+    for c in x_copies:
+        c.start()
+
+    for c in const_copies:
+        c.wait()
+    out_copies = []
+    for k in range(3):
+        h = gh_ref[k].reshape(depth * (rows + 2 * GHALO), wide)
+        l = gl_ref[k].reshape(depth * (rows + 2 * GHALO), wide)
+        t = dot(h, yh[...]) + dot(l, yh[...]) + dot(h, yl[...])
+        h, l = split2(t)
+        o = dot(xh[...], h) + dot(xh[...], l) + dot(xl[...], h)
+        out[k] = o.reshape(depth, rows, cols)
+        copy = pltpu.make_async_copy(out.at[k], out_hbm.at[k], out_sem.at[k])
+        copy.start()
+        out_copies.append(copy)
+
+    for c in x_copies:
+        c.wait()
+    total = part[1]
+    for d in range(1, nx):
+        total = total + by_x[d]
+    tissue_total = jnp.max(total[8:16], keepdims=True)
+    loss_ref[...] = -jnp.sum(total[0:8], keepdims=True) / (
+        tissue_total * float(BX * BY * depth)
+    )
+    for c in out_copies:
+        c.wait()
     for cs in (m_copies, f_copies, w_copies, s_copies):
         wait_send(cs)
-
-
-def smooth_kernel(gh_ref, gl_ref, yh_ref, yl_ref, xh_ref, xl_ref, out_ref):
-    _, depth, rows, wide = gh_ref.shape
-    h = gh_ref[...].reshape(depth * rows, wide)
-    l = gl_ref[...].reshape(depth * rows, wide)
-    t = dot(h, yh_ref[...]) + dot(l, yh_ref[...]) + dot(h, yl_ref[...])
-    h, l = split2(t)
-    o = dot(xh_ref[...], h) + dot(xh_ref[...], l) + dot(xl_ref[...], h)
-    out_ref[...] = o.reshape(out_ref.shape)
 
 
 def gauss():
@@ -404,12 +474,17 @@
 
     vmem = pl.BlockSpec(memory_space=pltpu.VMEM)
     smem = pl.BlockSpec(memory_space=pltpu.SMEM)
-    gshape = jax.ShapeDtypeStruct((3, depth, gext, wide), BF16)
-    gh, gl, acc = pl.pallas_call(
+    gshape = (3, depth, gext, wide)
+    hbm = pl.BlockSpec(memory_space=pl.ANY)
+    consts = gauss_y(cols) + gauss_zx(depth, rows)
+    update, loss = pl.pallas_call(
         functools.partial(fused_kernel, nx, ny),
-        out_shape=(gshape, gshape, jax.ShapeDtypeStruct((ext, wide), F32)),
-        in_specs=[smem, smem, vmem, vmem, pl.BlockSpec(memory_space=pl.ANY)],
-        out_specs=(vmem, vmem, vmem),
+        out_shape=(
+            jax.ShapeDtypeStruct((3, depth, rows, cols), F32),
+            jax.ShapeDtypeStruct((1, 1), F32),
+        ),
+        in_specs=[smem, smem, vmem, vmem, hbm, hbm, hbm, hbm, hbm],
+        out_specs=(hbm, vmem),
         scratch_shapes=[
             *ring(depth), *ring(depth + 1), *ring(depth), *ring(3 * depth),
             pltpu.VMEM(velocity.shape, F32),
@@ -419,32 +494,29 @@
             pltpu.VMEM((3, depth + 2 * BOX, ext, wide), F32),
             pltpu.VMEM((wide, wide), BF16),
             pltpu.VMEM((GROUP * ext, GROUP * ext), BF16),
+            pltpu.VMEM(gshape, BF16),
+            pltpu.VMEM(gshape, BF16),
+            pltpu.VMEM((3, depth, rows, cols), F32),
+            *[pltpu.VMEM(c.shape, BF16) for c in consts],
+            pltpu.VMEM((ext, wide), F32),
+            pltpu.VMEM((2, 16, BY), F32),
+            pltpu.VMEM((ny, 16, BY), F32),
+            pltpu.VMEM((nx, 16, BY), F32),
             pltpu.SemaphoreType.DMA,
+            pltpu.SemaphoreType.DMA((4,)),
+            pltpu.SemaphoreType.DMA((3,)),
             pltpu.SemaphoreType.DMA((4, 8)),
             pltpu.SemaphoreType.DMA((4, 8)),
+            pltpu.SemaphoreType.DMA((ny,)),
+            pltpu.SemaphoreType.DMA((ny,)),
+            pltpu.SemaphoreType.DMA((nx,)),
+            pltpu.SemaphoreType.DMA((nx,)),
         ],
         compiler_params=pltpu.CompilerParams(
             collective_id=0, has_side_effects=True, vmem_limit_bytes=56 * 2**20
         ),
-    )(offsets, tissue, moving, fixed, velocity)
-    totals = lax.psum(
-        jnp.stack([jnp.sum(acc), jnp.sum(tissue).astype(F32)]), ("gx", "gy")
-    )
-    loss = -totals[0] / (totals[1] * float(BX * BY * depth))
-
-    yh, yl = gauss_y(cols)
-    xh, xl = gauss_zx(depth, rows)
-    gspec = pl.BlockSpec((1, depth, gext, wide), lambda k: (k, 0, 0, 0))
-    whole = lambda a: pl.BlockSpec(a.shape, lambda k: (0, 0))
-    update = pl.pallas_call(
-        smooth_kernel,
-        grid=(3,),
-        out_shape=jax.ShapeDtypeStruct((3, depth, rows, cols), F32),
-        in_specs=[gspec, gspec, whole(yh), whole(yl), whole(xh), whole(xl)],
-        out_specs=pl.BlockSpec((1, depth, rows, cols), lambda k: (k, 0, 0, 0)),
-        compiler_params=pltpu.CompilerParams(vmem_limit_bytes=48 * 2**20),
-    )(gh, gl, jnp.asarray(yh), jnp.asarray(yl), jnp.asarray(xh), jnp.asarray(xl))
-    return update, loss
+    )(offsets, tissue, moving, fixed, velocity, *[jnp.asarray(c) for c in consts])
+    return update, loss[0, 0]
 
 
 def solution(mesh):

time: 138 us -> 88.4 us (0.64)
  the two profiles are of different devices: /device:TPU:0 before, /device:TPU:9 now
where the time goes in v1:
time: 88.4 us; the launch traced here: 87.6 us
  Pallas kernels  81.1 us (92%)
  local copies, waits for them, and re-layouts  4.07 us (5%)
  between operations  2.4 us (3%)
    pallas_call x1, Pallas kernels, on_device(): pl.pallas_call(functools.partial(fused_kernel, nx, ny), out_shape=(jax.Sh...  81.1 us
    unnamed x2, local copies, waits for them, and re-layouts  4.07 us

profile of v1, /device:TPU:9, one launch (start us, length us, event | category | flops | bytes accessed | tf_op | source)
XLA Modules:
  0.0 87.6 jit_solution(16616138013950018019)
XLA Ops:
  0.6 1.3 %copy.11.off_ref = s32[3,2,2]{2,1,0:T(2,128)} copy(s32[3,2,2]{0,2,1:T(2,128)} %param.12) | data formatting | bytes 96 | tf_op args[3]
  2.0 81.1 %shard_map.104 = (f32[3,16,32,256]{3,2,1,0:T(8,128)}, f32[1,1]{1,0:T(1,128)}) custom-call(s32[3,2,2]{2,1,0:T(2,128)} %copy.11.off_ref, s32[2,2]{1,0:T(2,128)} %tis_ref.1, bf16[16,32,256]{2,1,0:T(8,128)(2,1)} %mov_ref.1, bf16[16,32,256]{2,1,0:T(8,128)(2,1)} %fix_ref.1, f32[3,16,32,256]{3,2,1,0:T(8,128)} %vel_hbm.1, bf16[384,256]{1,0:T(8,128)(2,1)} %constant.8.clone.yh_hbm, ...), custom_call_target="tpu_custom_call" | custom-call | tf_op jit(solution)/shard_map/pallas_call | solution.py:480
  83.1 2.7 %copy.14 = f32[3,16,32,256]{3,2,1,0:T(8,128)} copy(f32[3,16,32,256]{3,2,1,0:T(8,128)} %get-tuple-element.8) | data formatting | bytes 3145728

commit v2 on v1

--- a/solution.py
+++ b/solution.py
@@ -20,6 +20,7 @@
 STEP_RATE = 16.0
 HALO = 16
 GHALO = 8
+PACK = BY // HALO
 GROUP = 4
 F32 = jnp.float32
 BF16 = jnp.bfloat16
@@ -44,27 +45,83 @@
     return h, m, (r - m.astype(F32)).astype(BF16)
 
 
-def halo_refs(direction, rows, center, left, right):
+def halo_refs(direction, rows, center, to_left, to_right, left, right):
     dx, dy = direction
-    src_rows = {-1: pl.ds(HALO, HALO), 0: pl.ds(HALO, rows), 1: pl.ds(rows, HALO)}[dx]
+    cols = center.shape[2] - BY
     dst_rows = {-1: pl.ds(HALO + rows, HALO), 0: pl.ds(HALO, rows), 1: pl.ds(0, HALO)}[dx]
-    cols = center.shape[2]
     if dy == 0:
-        return center.at[:, src_rows, :], center.at[:, dst_rows, :]
+        src_rows = pl.ds(HALO, HALO) if dx < 0 else pl.ds(rows, HALO)
+        own = pl.ds(0, cols)
+        return center.at[:, src_rows, own], center.at[:, dst_rows, own]
+    src_rows = {-1: pl.ds(0, HALO), 0: pl.ds(0, rows), 1: pl.ds(rows - HALO, HALO)}[dx]
     if dy < 0:
-        return center.at[:, src_rows, pl.ds(0, BY)], right.at[:, dst_rows, :]
-    return center.at[:, src_rows, pl.ds(cols - BY, BY)], left.at[:, dst_rows, :]
+        return to_left.at[:, src_rows, :], right.at[:, dst_rows, :]
+    return to_right.at[:, src_rows, :], left.at[:, dst_rows, :]
+
+
+def groups_of(planes, body):
+    def step(g, carry):
+        body(g * PACK, g, PACK)
+        return carry
+
+    lax.fori_loop(0, planes // PACK, step, 0)
+    if planes % PACK:
+        body(planes - planes % PACK, planes // PACK, planes % PACK)
+
+
+def turn(x, shift, axis):
+    shift %= x.shape[axis]
+    return x if shift == 0 else pltpu.roll(x, shift, axis)
+
+
+def pack(center, to_left, to_right, rows):
+    cols = center.shape[2] - BY
+    lane = lax.broadcasted_iota(jnp.int32, (rows, BY), 1)
+
+    def body(z, g, count):
+        l = jnp.zeros((rows, BY), F32)
+        r = jnp.zeros((rows, BY), F32)
+        for i in range(count):
+            mine = jnp.logical_and(lane >= i * HALO, lane < (i + 1) * HALO)
+            a = center[z + i, HALO : HALO + rows, 0:BY].astype(F32)
+            b = center[z + i, HALO : HALO + rows, cols - BY : cols].astype(F32)
+            l = jnp.where(mine, turn(a, i * HALO, 1), l)
+            r = jnp.where(mine, turn(b, (i + 1) * HALO, 1), r)
+        to_left[g] = l.astype(BF16)
+        to_right[g] = r.astype(BF16)
+
+    groups_of(center.shape[0], body)
+
+
+def unpack(center, left, right):
+    _, ext, wide = center.shape
+    lane = lax.broadcasted_iota(jnp.int32, (ext, BY), 1)
+
+    def body(z, g, count):
+        l, r = left[g].astype(F32), right[g].astype(F32)
+        for i in range(count):
+            v = jnp.where(lane < HALO, turn(r, -i * HALO, 1), 0.0)
+            v = jnp.where(lane >= BY - HALO, turn(l, -(i + 1) * HALO, 1), v)
+            center[z + i, :, wide - BY : wide] = v.astype(BF16)
+
+    groups_of(center.shape[0], body)
+
+
+def window_x(v):
+    s = v + turn(v, 1, 0) + turn(v, -1, 0)
+    return s + turn(s, 3, 0) + turn(s, -3, 0)
 
 
 def fused_kernel(
     nx, ny,
     off_ref, tis_ref, mov_ref, fix_ref, vel_hbm, yh_hbm, yl_hbm, xh_hbm, xl_hbm,
     out_hbm, loss_ref,
-    mC, mL, mR, fC, fL, fR, wC, wL, wR, sC, sL, sR,
-    vel, sF, T, Y, A, by_ref, bx_ref,
-    gh_ref, gl_ref, out, yh, yl, xh, xl, acc_ref, part, by_y, by_x,
+    m, f, w, s,
+    vel, sF, T, Y, A, by_ref,
+    gh_ref, gl_ref, out, yh, yl, xh, xl, acc_ref, mask_ref, own_ref, part, by_y, by_x,
     vel_sem, const_sem, out_sem, send_sem, recv_sem, ysend_sem, yrecv_sem, xsend_sem, xrecv_sem,
 ):
+    (mC, fC, wC, sC) = (m[0], f[0], w[0], s[0])
     depth, rows, cols = mov_ref.shape
     ext = rows + 2 * HALO
     wide = cols + BY
@@ -107,24 +164,25 @@
             barrier, inc=1, device_id=(lax.rem(gx + d, nx), gy), device_id_type=MESH
         )
 
-    def clear(center, left, right):
+    def clear(*bufs):
         for i, (dx, dy) in enumerate(DIRS):
-            _, dst = halo_refs((-dx, -dy), rows, center, left, right)
+            _, dst = halo_refs((-dx, -dy), rows, *bufs)
 
             @pl.when(jnp.logical_not(has[i]))
             def _():
                 dst[...] = jnp.zeros(dst.shape, dst.dtype)
 
-    mC[:, HALO : HALO + rows, :] = mov_ref[...]
+    mC[:, HALO : HALO + rows, 0:cols] = mov_ref[...]
+    pack(m[0], m[1], m[2], rows)
     def line(g, n):
         return 1 + jnp.where(g > 0, 1, 0) + jnp.where(g < n - 1, 1, 0)
 
     pl.semaphore_wait(barrier, line(gx, nx) * line(gy, ny) - 1 + (ny - 1) + (nx - 1))
 
-    def copies(t, center, left, right):
+    def copies(t, *bufs):
         out = []
         for i, (dx, dy) in enumerate(DIRS):
-            src, dst = halo_refs((dx, dy), rows, center, left, right)
+            src, dst = halo_refs((dx, dy), rows, *bufs)
             out.append(
                 pltpu.make_async_remote_copy(
                     src_ref=src, dst_ref=dst,
@@ -154,38 +212,32 @@
             def _():
                 c.wait_send()
 
-    m_copies = copies(0, mC, mL, mR)
-    f_copies = copies(1, fC, fL, fR)
-    w_copies = copies(2, wC, wL, wR)
-    s_copies = copies(3, sC, sL, sR)
+    m_copies = copies(0, *m)
+    f_copies = copies(1, *f)
+    w_copies = copies(2, *w)
+    s_copies = copies(3, *s)
     start(m_copies)
 
-    fC[0:depth, HALO : HALO + rows, :] = fix_ref[...]
+    fC[0:depth, HALO : HALO + rows, 0:cols] = fix_ref[...]
     for r in range(rows // BX):
         for c in range(cols // BY):
             value = tis_ref[r, c].astype(F32)
             fC[depth, HALO + r * BX : HALO + (r + 1) * BX, c * BY : (c + 1) * BY] = jnp.full(
                 (BX, BY), value, F32
             ).astype(BF16)
+    pack(f[0], f[1], f[2], rows)
     start(f_copies)
 
-    clear(mC, mL, mR)
-    clear(fC, fL, fR)
-    clear(wC, wL, wR)
-    clear(sC, sL, sR)
+    clear(*m)
+    clear(*f)
+    clear(*w)
+    clear(*s)
 
     ki = lax.broadcasted_iota(jnp.int32, (wide, wide), 0)
     ji = lax.broadcasted_iota(jnp.int32, (wide, wide), 1)
     dist = jnp.abs(ki - ji)
     dist = jnp.minimum(dist, wide - dist)
     by_ref[...] = jnp.where(dist <= BOX, 1.0, 0.0).astype(BF16)
-    size = GROUP * ext
-    ki = lax.broadcasted_iota(jnp.int32, (size, size), 0)
-    ji = lax.broadcasted_iota(jnp.int32, (size, size), 1)
-    same = (ki // ext) == (ji // ext)
-    bx_ref[...] = jnp.where(
-        jnp.logical_and(same, jnp.abs(ki - ji) <= BOX), 1.0, 0.0
-    ).astype(BF16)
     zpad = ZREACH + 1
     T[0:zpad] = jnp.zeros((zpad,) + T.shape[1:], F32)
     T[depth + zpad :] = jnp.zeros((zpad,) + T.shape[1:], F32)
@@ -196,15 +248,8 @@
         A[k, 0:BOX] = jnp.zeros((BOX, ext, wide), F32)
         A[k, depth + BOX :] = jnp.zeros((BOX, ext, wide), F32)
 
-    def side(left, right):
-        lane = lax.broadcasted_iota(jnp.int32, left.shape, left.ndim - 1)
-        return jnp.where(lane < BY // 2, right.astype(F32), left.astype(F32))
-
-    def joined(center, left, right):
-        s = side(left, right).astype(center.dtype)
-        return jnp.concatenate([center, s], axis=-1)
-
     wait_recv(m_copies)
+    unpack(m[0], m[3], m[4])
     vel_copy.wait()
 
     slab = BX + 2 * HALO
@@ -224,11 +269,7 @@
 
             def move(g, carry):
                 z = pl.multiple_of(g * GROUP, GROUP)
-                x = joined(
-                    mC[pl.ds(z, GROUP), r0 : r0 + slab, :],
-                    mL[pl.ds(z, GROUP), r0 : r0 + slab, :],
-                    mR[pl.ds(z, GROUP), r0 : r0 + slab, :],
-                )
+                x = mC[pl.ds(z, GROUP), r0 : r0 + slab, :]
                 t = dot(x.reshape(GROUP * slab, wide), shift).astype(BF16)
                 T[pl.ds(z + zpad, GROUP)] = dot(down, t).reshape(GROUP, 2 * BX, 2 * BY)
                 return carry
@@ -266,23 +307,35 @@
 
             lax.fori_loop(0, depth, warp, 0)
 
+    pack(w[0], w[1], w[2], rows)
     start(w_copies)
+    pack(s[0], s[1], s[2], rows)
     start(s_copies)
     wait_recv(f_copies)
+    unpack(f[0], f[3], f[4])
+
+    by = by_ref[...]
+
+    def fixed_y(g, carry):
+        z = g * GROUP
+        j_low = fC[pl.ds(z, GROUP)].reshape(GROUP * ext, wide)
+        j = j_low.astype(F32)
+        h, l = split2(j * j)
+        Y[1, pl.ds(z + BOX, GROUP)] = dot(j_low, by).reshape(GROUP, ext, wide)
+        Y[3, pl.ds(z + BOX, GROUP)] = (dot(h, by) + dot(l, by)).reshape(GROUP, ext, wide)
+        return carry
+
+    lax.fori_loop(0, depth // GROUP, fixed_y, 0)
     wait_recv(w_copies)
-
-    by = by_ref[...]
-
-    def image(center, left, right, z):
-        return joined(center[pl.ds(z, GROUP)], left[pl.ds(z, GROUP)], right[pl.ds(z, GROUP)])
+    unpack(w[0], w[3], w[4])
 
     def stats_y(g, carry):
         z = g * GROUP
-        i_low = image(wC, wL, wR, z).reshape(GROUP * ext, wide)
-        j_low = image(fC, fL, fR, z).reshape(GROUP * ext, wide)
-        i, j = i_low.astype(F32), j_low.astype(F32)
-        fields = [(i_low,), (j_low,), split2(i * i), split2(j * j), split2(i * j)]
-        for k, parts in enumerate(fields):
+        i_low = wC[pl.ds(z, GROUP)].reshape(GROUP * ext, wide)
+        i = i_low.astype(F32)
+        j = fC[pl.ds(z, GROUP)].reshape(GROUP * ext, wide).astype(F32)
+        fields = [(0, (i_low,)), (2, split2(i * i)), (4, split2(i * j))]
+        for k, parts in fields:
             y = dot(parts[0], by)
             for part in parts[1:]:
                 y = y + dot(part, by)
@@ -291,43 +344,50 @@
 
     lax.fori_loop(0, depth // GROUP, stats_y, 0)
 
-    def window_z(ref, k, z):
-        p = [ref[k, z + t] for t in range(GROUP + 2 * BOX)]
+    def window_z(ref, k, z, tile):
+        p = [ref[k, z + t, :, tile] for t in range(GROUP + 2 * BOX)]
         common = ((p[3] + p[4]) + (p[5] + p[6])) + (p[7] + p[8])
         low, high = p[1] + p[2], p[9] + p[10]
         outs = [
             common + (p[0] + low), common + (low + p[9]),
             common + (p[2] + high), common + (high + p[11]),
         ]
-        return jnp.concatenate(outs, axis=0)
-
-    mask = joined(fC[depth], fL[depth], fR[depth]).astype(F32)
+        return window_x(jnp.concatenate(outs, axis=0))
+
+    tiles = [slice(c, c + BY) for c in range(0, wide, BY)]
+
     row = lax.broadcasted_iota(jnp.int32, (ext, wide), 0)
     lane = lax.broadcasted_iota(jnp.int32, (ext, wide), 1)
-    own = jnp.logical_and(jnp.logical_and(row >= HALO, row < HALO + rows), lane < cols)
-    own_mask = jnp.where(own, mask, 0.0)
+    own_row = jnp.logical_and(row >= HALO, row < HALO + rows)
     acc_ref[...] = jnp.zeros_like(acc_ref)
+    reach = HALO - BOX - 1
+    near = jnp.logical_and(row >= HALO - reach, row < HALO + rows + reach)
+    near = jnp.logical_and(near, jnp.logical_or(lane < cols + reach, lane >= wide - reach))
+    mask_ref[...] = jnp.where(near, fC[depth].astype(F32), 0.0)
+    own_ref[...] = jnp.where(jnp.logical_and(own_row, lane < cols), mask_ref[...], 0.0)
 
     def stats(g, carry):
         z = g * GROUP
-        sums = []
-        for k in range(5):
-            h, m, l = split3(window_z(Y, k, z))
-            sums.append(dot(bx_ref[...], h) + dot(bx_ref[...], m) + dot(bx_ref[...], l))
-        si, sj, sii, sjj, sij = [s.reshape(GROUP, ext, wide) for s in sums]
-        cross = sij - si * sj * (1.0 / COUNT)
-        var_i = sii - si * si * (1.0 / COUNT)
-        var_j = sjj - sj * sj * (1.0 / COUNT)
-        q = cross / (var_i * var_j + EPS)
-        live = mask[None] > 0.0
-        acc_ref[...] += jnp.sum(jnp.where(own_mask[None] > 0.0, cross * q, 0.0), axis=0)
-        q = jnp.where(live, q, 0.0)
-        p = jnp.where(live, q * q * var_j, 0.0)
-        terms = (
-            jnp.where(live, (2.0 / COUNT) * (q * sj - p * si), 0.0), p, -2.0 * q,
-        )
+        terms = [[], [], []]
+        for tile in tiles:
+            si, sj, sii, sjj, sij = [
+                window_z(Y, k, z, tile).reshape(GROUP, ext, BY) for k in range(5)
+            ]
+            cross = sij - si * sj * (1.0 / COUNT)
+            var_i = sii - si * si * (1.0 / COUNT)
+            var_j = sjj - sj * sj * (1.0 / COUNT)
+            q = cross / (var_i * var_j + EPS)
+            live = mask_ref[:, tile][None] > 0.0
+            if tile.start < cols:
+                own = own_ref[:, tile][None] > 0.0
+                acc_ref[:, tile] += jnp.sum(jnp.where(own, cross * q, 0.0), axis=0)
+            q = jnp.where(live, q, 0.0)
+            p = q * q * var_j
+            values = ((2.0 / COUNT) * (q * sj - p * si), p, -2.0 * q)
+            for k in range(3):
+                terms[k].append(values[k].reshape(GROUP * ext, BY))
         for k in range(3):
-            h, l = split2(terms[k].reshape(GROUP * ext, wide))
+            h, l = split2(jnp.concatenate(terms[k], axis=1))
             y = dot(h, by_ref[...]) + dot(l, by_ref[...])
             A[k, pl.ds(z + BOX, GROUP)] = y.reshape(GROUP, ext, wide)
         return carry
@@ -364,28 +424,29 @@
         c.start()
 
     wait_recv(s_copies)
+    unpack(s[0], s[3], s[4])
     inner = slice(HALO - GHALO, HALO + rows + GHALO)
 
     def grads(g, carry):
         z = g * GROUP
-        box = []
-        for k in range(3):
-            h, l = split2(window_z(A, k, z))
-            b = dot(bx_ref[...], h) + dot(bx_ref[...], l)
-            box.append(b.reshape(GROUP, ext, wide)[:, inner])
-        i = image(wC, wL, wR, z).astype(F32)[:, inner]
-        j = image(fC, fL, fR, z).astype(F32)[:, inner]
-        grad = box[0] + 2.0 * i * box[1] + j * box[2]
-        for k in range(3):
-            zs = pl.ds(k * depth + z, GROUP)
-            c = sC[zs].astype(F32)
-            c = jnp.concatenate(
-                [c[:, HALO - GHALO : HALO], sF[k, pl.ds(z, GROUP)],
-                 c[:, HALO + rows : HALO + rows + GHALO]], axis=1)
-            s = side(sL[zs], sR[zs])[:, inner]
-            h, l = split2(grad * jnp.concatenate([c, s], axis=-1))
-            gh_ref[k, pl.ds(z, GROUP)] = h
-            gl_ref[k, pl.ds(z, GROUP)] = l
+        for tile in tiles:
+            box = [
+                window_z(A, k, z, tile).reshape(GROUP, ext, BY)[:, inner] for k in range(3)
+            ]
+            i = wC[pl.ds(z, GROUP), :, tile].astype(F32)[:, inner]
+            j = fC[pl.ds(z, GROUP), :, tile].astype(F32)[:, inner]
+            grad = box[0] + 2.0 * i * box[1] + j * box[2]
+            for k in range(3):
+                c = sC[pl.ds(k * depth + z, GROUP), :, tile].astype(F32)
+                if tile.start < cols:
+                    c = jnp.concatenate(
+                        [c[:, HALO - GHALO : HALO], sF[k, pl.ds(z, GROUP), :, tile],
+                         c[:, HALO + rows : HALO + rows + GHALO]], axis=1)
+                else:
+                    c = c[:, inner]
+                h, l = split2(grad * c)
+                gh_ref[k, pl.ds(z, GROUP), :, tile] = h
+                gl_ref[k, pl.ds(z, GROUP), :, tile] = l
         return carry
 
     lax.fori_loop(0, depth // GROUP, grads, 0)
@@ -466,11 +527,14 @@
     ext, wide, gext = rows + 2 * HALO, cols + BY, rows + 2 * GHALO
 
     def ring(n):
-        return [
-            pltpu.VMEM((n, ext, cols), BF16),
-            pltpu.VMEM((n, ext, BY), BF16),
-            pltpu.VMEM((n, ext, BY), BF16),
-        ]
+        packs = -(-n // PACK)
+        return (
+            pltpu.VMEM((n, ext, wide), BF16),
+            pltpu.VMEM((packs, rows, BY), BF16),
+            pltpu.VMEM((packs, rows, BY), BF16),
+            pltpu.VMEM((packs, ext, BY), BF16),
+            pltpu.VMEM((packs, ext, BY), BF16),
+        )
 
     vmem = pl.BlockSpec(memory_space=pltpu.VMEM)
     smem = pl.BlockSpec(memory_space=pltpu.SMEM)
@@ -486,18 +550,19 @@
         in_specs=[smem, smem, vmem, vmem, hbm, hbm, hbm, hbm, hbm],
         out_specs=(hbm, vmem),
         scratch_shapes=[
-            *ring(depth), *ring(depth + 1), *ring(depth), *ring(3 * depth),
+            ring(depth), ring(depth + 1), ring(depth), ring(3 * depth),
             pltpu.VMEM(velocity.shape, F32),
             pltpu.VMEM((3, depth, rows, cols), F32),
             pltpu.VMEM((depth + 2 * (ZREACH + 1), 2 * BX, 2 * BY), F32),
             pltpu.VMEM((5, depth + 2 * BOX, ext, wide), F32),
             pltpu.VMEM((3, depth + 2 * BOX, ext, wide), F32),
             pltpu.VMEM((wide, wide), BF16),
-            pltpu.VMEM((GROUP * ext, GROUP * ext), BF16),
             pltpu.VMEM(gshape, BF16),
             pltpu.VMEM(gshape, BF16),
             pltpu.VMEM((3, depth, rows, cols), F32),
             *[pltpu.VMEM(c.shape, BF16) for c in consts],
+            pltpu.VMEM((ext, wide), F32),
+            pltpu.VMEM((ext, wide), F32),
             pltpu.VMEM((ext, wide), F32),
             pltpu.VMEM((2, 16, BY), F32),
             pltpu.VMEM((ny, 16, BY), F32),

time: 88.4 us -> 73.6 us (0.83)
  Pallas kernels: 81.1 us -> 67 us
    pallas_call x1, Pallas kernels: 81.1 us -> 67 us  [on_device(): pl.pallas_call(functools.partial(fused_kernel, nx, ny), out_shape=(jax.Sh...]
where the time goes in v2:
time: 73.6 us; the launch traced here: 73.4 us
  Pallas kernels  67 us (91%)
  local copies, waits for them, and re-layouts  4.07 us (6%)
  between operations  2.4 us (3%)
    pallas_call x1, Pallas kernels, on_device(): pl.pallas_call(functools.partial(fused_kernel, nx, ny), out_shape=(jax.Sh...  67 us
    unnamed x2, local copies, waits for them, and re-layouts  4.07 us

profile of v2, /device:TPU:9, one launch (start us, length us, event | category | flops | bytes accessed | tf_op | source)
XLA Modules:
  0.0 73.4 jit_solution(1609836857134154069)
XLA Ops:
  0.6 1.3 %copy.11.off_ref = s32[3,2,2]{2,1,0:T(2,128)} copy(s32[3,2,2]{0,2,1:T(2,128)} %param.12) | data formatting | bytes 96 | tf_op args[3]
  2.0 67.0 %shard_map.104 = (f32[3,16,32,256]{3,2,1,0:T(8,128)}, f32[1,1]{1,0:T(1,128)}) custom-call(s32[3,2,2]{2,1,0:T(2,128)} %copy.11.off_ref, s32[2,2]{1,0:T(2,128)} %tis_ref.1, bf16[16,32,256]{2,1,0:T(8,128)(2,1)} %mov_ref.1, bf16[16,32,256]{2,1,0:T(8,128)(2,1)} %fix_ref.1, f32[3,16,32,256]{3,2,1,0:T(8,128)} %vel_hbm.1, bf16[384,256]{1,0:T(8,128)(2,1)} %constant.8.clone.yh_hbm, ...), custom_call_target="tpu_custom_call" | custom-call | tf_op jit(solution)/shard_map/pallas_call | solution.py:544
  68.9 2.7 %copy.14 = f32[3,16,32,256]{3,2,1,0:T(8,128)} copy(f32[3,16,32,256]{3,2,1,0:T(8,128)} %get-tuple-element.8) | data formatting | bytes 3145728

commit v3 on v2

--- a/solution.py
+++ b/solution.py
@@ -3,7 +3,6 @@
 
 import jax
 import jax.numpy as jnp
-import numpy as np
 from jax import lax
 from jax.experimental import pallas as pl
 from jax.experimental.pallas import tpu as pltpu
@@ -45,10 +44,13 @@
     return h, m, (r - m.astype(F32)).astype(BF16)
 
 
-def halo_refs(direction, rows, center, to_left, to_right, left, right):
+def halo_refs(direction, rows, center, to_left, to_right, left, right, *thin):
     dx, dy = direction
     cols = center.shape[2] - BY
     dst_rows = {-1: pl.ds(HALO + rows, HALO), 0: pl.ds(HALO, rows), 1: pl.ds(0, HALO)}[dx]
+    if dy == 0 and thin:
+        up, down, top, bottom = thin
+        return (up, bottom) if dx < 0 else (down, top)
     if dy == 0:
         src_rows = pl.ds(HALO, HALO) if dx < 0 else pl.ds(rows, HALO)
         own = pl.ds(0, cols)
@@ -93,6 +95,42 @@
     groups_of(center.shape[0], body)
 
 
+def pack_rows(center, up, down, rows):
+    cols = center.shape[2] - BY
+
+    def body(g, carry):
+        for i in range(4):
+            h = g * 4 + i
+            a = center[2 * h, HALO : HALO + rows, 0:cols].astype(F32)
+            b = center[2 * h + 1, HALO : HALO + rows, 0:cols].astype(F32)
+            up[h] = jnp.concatenate([a[:GHALO], b[:GHALO]], axis=0).astype(BF16)
+            down[h] = jnp.concatenate([a[-GHALO:], b[-GHALO:]], axis=0).astype(BF16)
+        return carry
+
+    lax.fori_loop(0, center.shape[0] // 8, body, 0)
+
+
+def unpack_rows(center, top, bottom, rows):
+    cols = center.shape[2] - BY
+    none = jnp.zeros((HALO - GHALO, cols), F32)
+
+    def body(g, carry):
+        for i in range(4):
+            h = g * 4 + i
+            t, b = top[h].astype(F32), bottom[h].astype(F32)
+            for j in range(2):
+                part = slice(j * GHALO, (j + 1) * GHALO)
+                center[2 * h + j, 0:HALO, 0:cols] = jnp.concatenate(
+                    [none, t[part]], axis=0
+                ).astype(BF16)
+                center[2 * h + j, HALO + rows : 2 * HALO + rows, 0:cols] = jnp.concatenate(
+                    [b[part], none], axis=0
+                ).astype(BF16)
+        return carry
+
+    lax.fori_loop(0, center.shape[0] // 8, body, 0)
+
+
 def unpack(center, left, right):
     _, ext, wide = center.shape
     lane = lax.broadcasted_iota(jnp.int32, (ext, BY), 1)
@@ -114,12 +152,12 @@
 
 def fused_kernel(
     nx, ny,
-    off_ref, tis_ref, mov_ref, fix_ref, vel_hbm, yh_hbm, yl_hbm, xh_hbm, xl_hbm,
+    off_ref, tis_ref, mov_ref, fix_ref, vel_hbm,
     out_hbm, loss_ref,
     m, f, w, s,
     vel, sF, T, Y, A, by_ref,
     gh_ref, gl_ref, out, yh, yl, xh, xl, acc_ref, mask_ref, own_ref, part, by_y, by_x,
-    vel_sem, const_sem, out_sem, send_sem, recv_sem, ysend_sem, yrecv_sem, xsend_sem, xrecv_sem,
+    vel_sem, out_sem, send_sem, recv_sem, ysend_sem, yrecv_sem, xsend_sem, xrecv_sem,
 ):
     (mC, fC, wC, sC) = (m[0], f[0], w[0], s[0])
     depth, rows, cols = mov_ref.shape
@@ -142,13 +180,6 @@
 
     vel_copy = pltpu.make_async_copy(vel_hbm, vel, vel_sem)
     vel_copy.start()
-    const_copies = [
-        pltpu.make_async_copy(a, b, const_sem.at[i])
-        for i, (a, b) in enumerate(((yh_hbm, yh), (yl_hbm, yl), (xh_hbm, xh), (xl_hbm, xl)))
-    ]
-    for c in const_copies:
-        c.start()
-
     barrier = pltpu.get_barrier_semaphore()
     for i, (dx, dy) in enumerate(DIRS):
         @pl.when(has[i])
@@ -173,6 +204,7 @@
                 dst[...] = jnp.zeros(dst.shape, dst.dtype)
 
     mC[:, HALO : HALO + rows, 0:cols] = mov_ref[...]
+    pack_rows(m[0], m[5], m[6], rows)
     pack(m[0], m[1], m[2], rows)
     def line(g, n):
         return 1 + jnp.where(g > 0, 1, 0) + jnp.where(g < n - 1, 1, 0)
@@ -238,6 +270,7 @@
     dist = jnp.abs(ki - ji)
     dist = jnp.minimum(dist, wide - dist)
     by_ref[...] = jnp.where(dist <= BOX, 1.0, 0.0).astype(BF16)
+    yh[...], yl[...] = gauss_y(wide, cols)
     zpad = ZREACH + 1
     T[0:zpad] = jnp.zeros((zpad,) + T.shape[1:], F32)
     T[depth + zpad :] = jnp.zeros((zpad,) + T.shape[1:], F32)
@@ -249,6 +282,7 @@
         A[k, depth + BOX :] = jnp.zeros((BOX, ext, wide), F32)
 
     wait_recv(m_copies)
+    unpack_rows(m[0], m[7], m[8], rows)
     unpack(m[0], m[3], m[4])
     vel_copy.wait()
 
@@ -305,10 +339,16 @@
                     sC[k * depth + z, hs, cs] = slopes[k].astype(BF16)
                 return carry
 
-            lax.fori_loop(0, depth, warp, 0)
+            def warp_group(g, carry):
+                for t in range(GROUP):
+                    warp(g * GROUP + t, carry)
+                return carry
+
+            lax.fori_loop(0, depth // GROUP, warp_group, 0)
 
     pack(w[0], w[1], w[2], rows)
     start(w_copies)
+    pack_rows(s[0], s[5], s[6], rows)
     pack(s[0], s[1], s[2], rows)
     start(s_copies)
     wait_recv(f_copies)
@@ -326,6 +366,8 @@
         return carry
 
     lax.fori_loop(0, depth // GROUP, fixed_y, 0)
+    for z in range(depth):
+        xh[z * rows : (z + 1) * rows], xl[z * rows : (z + 1) * rows] = gauss_zx(rows, depth, z)
     wait_recv(w_copies)
     unpack(w[0], w[3], w[4])
 
@@ -385,10 +427,9 @@
             p = q * q * var_j
             values = ((2.0 / COUNT) * (q * sj - p * si), p, -2.0 * q)
             for k in range(3):
-                terms[k].append(values[k].reshape(GROUP * ext, BY))
+                terms[k].append(values[k].reshape(GROUP * ext, BY).astype(BF16))
         for k in range(3):
-            h, l = split2(jnp.concatenate(terms[k], axis=1))
-            y = dot(h, by_ref[...]) + dot(l, by_ref[...])
+            y = dot(jnp.concatenate(terms[k], axis=1), by_ref[...])
             A[k, pl.ds(z + BOX, GROUP)] = y.reshape(GROUP, ext, wide)
         return carry
 
@@ -424,6 +465,7 @@
         c.start()
 
     wait_recv(s_copies)
+    unpack_rows(s[0], s[7], s[8], rows)
     unpack(s[0], s[3], s[4])
     inner = slice(HALO - GHALO, HALO + rows + GHALO)
 
@@ -460,8 +502,6 @@
     for c in x_copies:
         c.start()
 
-    for c in const_copies:
-        c.wait()
     out_copies = []
     for k in range(3):
         h = gh_ref[k].reshape(depth * (rows + 2 * GHALO), wide)
@@ -489,44 +529,40 @@
         wait_send(cs)
 
 
-def gauss():
-    taps = np.arange(-GAUSS_RADIUS, GAUSS_RADIUS + 1)
-    w = np.exp(-(taps * taps) / (2.0 * GAUSS_SIGMA**2))
-    return w / w.sum()
-
-
-def as_pair(m):
-    h = m.astype(jnp.bfloat16)
-    return h, (m - h.astype(np.float64)).astype(jnp.bfloat16)
-
-
-def gauss_y(cols):
-    w, wide = gauss(), cols + BY
-    m = np.zeros((wide, cols))
-    for j in range(cols):
-        for t in range(-GAUSS_RADIUS, GAUSS_RADIUS + 1):
-            m[(j + t) % wide, j] = w[t + GAUSS_RADIUS]
-    return as_pair(m)
-
-
-def gauss_zx(depth, rows):
-    w = gauss()
-    mx = np.zeros((rows, rows + 2 * GHALO))
-    mz = np.zeros((depth, depth))
-    for t in range(-GAUSS_RADIUS, GAUSS_RADIUS + 1):
-        for r in range(rows):
-            mx[r, r + GHALO + t] = w[t + GAUSS_RADIUS]
-        for z in range(depth):
-            if 0 <= z + t < depth:
-                mz[z, z + t] = w[t + GAUSS_RADIUS]
-    return as_pair(-STEP_RATE * np.kron(mz, mx))
+def gauss_scale():
+    taps = range(-GAUSS_RADIUS, GAUSS_RADIUS + 1)
+    return 1.0 / sum(math.exp(-float(t * t) / (2.0 * GAUSS_SIGMA**2)) for t in taps)
+
+
+def gauss_y(wide, cols):
+    k = lax.broadcasted_iota(jnp.int32, (wide, cols), 0)
+    j = lax.broadcasted_iota(jnp.int32, (wide, cols), 1)
+    d = jnp.abs(k - j)
+    d = jnp.minimum(d, wide - d)
+    t = d.astype(F32)
+    e = jnp.exp(t * t * (-0.5 / GAUSS_SIGMA**2)) * gauss_scale()
+    return split2(jnp.where(d <= GAUSS_RADIUS, e, 0.0))
+
+
+def gauss_zx(rows, depth, z):
+    gext = rows + 2 * GHALO
+    k = lax.broadcasted_iota(jnp.int32, (1, depth * gext), 1).astype(F32)
+    kz = jnp.floor((k + 0.5) * (1.0 / gext))
+    kx = k - kz * gext - GHALO
+    r = lax.broadcasted_iota(jnp.int32, (rows, 1), 0).astype(F32)
+    dz, dx = jnp.abs(kz - z), jnp.abs(kx - r)
+    far = jnp.where(dz > GAUSS_RADIUS, 1e4, dz * dz) + jnp.where(
+        dx > GAUSS_RADIUS, 1e4, dx * dx
+    )
+    e = jnp.exp(far * (-0.5 / GAUSS_SIGMA**2)) * (-STEP_RATE * gauss_scale() ** 2)
+    return split2(e)
 
 
 def on_device(nx, ny, moving, fixed, velocity, offsets, tissue):
     depth, rows, cols = moving.shape
     ext, wide, gext = rows + 2 * HALO, cols + BY, rows + 2 * GHALO
 
-    def ring(n):
+    def ring(n, thin=False):
         packs = -(-n // PACK)
         return (
             pltpu.VMEM((n, ext, wide), BF16),
@@ -534,23 +570,23 @@
             pltpu.VMEM((packs, rows, BY), BF16),
             pltpu.VMEM((packs, ext, BY), BF16),
             pltpu.VMEM((packs, ext, BY), BF16),
+            *[pltpu.VMEM((n // 2, 2 * GHALO, cols), BF16)] * (4 if thin else 0),
         )
 
     vmem = pl.BlockSpec(memory_space=pltpu.VMEM)
     smem = pl.BlockSpec(memory_space=pltpu.SMEM)
     gshape = (3, depth, gext, wide)
     hbm = pl.BlockSpec(memory_space=pl.ANY)
-    consts = gauss_y(cols) + gauss_zx(depth, rows)
     update, loss = pl.pallas_call(
         functools.partial(fused_kernel, nx, ny),
         out_shape=(
             jax.ShapeDtypeStruct((3, depth, rows, cols), F32),
             jax.ShapeDtypeStruct((1, 1), F32),
         ),
-        in_specs=[smem, smem, vmem, vmem, hbm, hbm, hbm, hbm, hbm],
+        in_specs=[smem, smem, vmem, vmem, hbm],
         out_specs=(hbm, vmem),
         scratch_shapes=[
-            ring(depth), ring(depth + 1), ring(depth), ring(3 * depth),
+            ring(depth, True), ring(depth + 1), ring(depth), ring(3 * depth, True),
             pltpu.VMEM(velocity.shape, F32),
             pltpu.VMEM((3, depth, rows, cols), F32),
             pltpu.VMEM((depth + 2 * (ZREACH + 1), 2 * BX, 2 * BY), F32),
@@ -560,7 +596,8 @@
             pltpu.VMEM(gshape, BF16),
             pltpu.VMEM(gshape, BF16),
             pltpu.VMEM((3, depth, rows, cols), F32),
-            *[pltpu.VMEM(c.shape, BF16) for c in consts],
+            *[pltpu.VMEM((wide, cols), BF16)] * 2,
+            *[pltpu.VMEM((depth * rows, depth * gext), BF16)] * 2,
             pltpu.VMEM((ext, wide), F32),
             pltpu.VMEM((ext, wide), F32),
             pltpu.VMEM((ext, wide), F32),
@@ -568,7 +605,6 @@
             pltpu.VMEM((ny, 16, BY), F32),
             pltpu.VMEM((nx, 16, BY), F32),
             pltpu.SemaphoreType.DMA,
-            pltpu.SemaphoreType.DMA((4,)),
             pltpu.SemaphoreType.DMA((3,)),
             pltpu.SemaphoreType.DMA((4, 8)),
             pltpu.SemaphoreType.DMA((4, 8)),
@@ -578,9 +614,9 @@
             pltpu.SemaphoreType.DMA((nx,)),
         ],
         compiler_params=pltpu.CompilerParams(
-            collective_id=0, has_side_effects=True, vmem_limit_bytes=56 * 2**20
+            collective_id=0, has_side_effects=True, vmem_limit_bytes=48 * 2**20
         ),
-    )(offsets, tissue, moving, fixed, velocity, *[jnp.asarray(c) for c in consts])
+    )(offsets, tissue, moving, fixed, velocity)
     return update, loss[0, 0]
 
 

time: 73.6 us -> 68.2 us (0.927)
  Pallas kernels: 67 us -> 59.6 us
  local copies, waits for them, and re-layouts: 4.07 us -> 5.9 us
    pallas_call x1, Pallas kernels: 67 us -> 59.6 us  [on_device(): pl.pallas_call(functools.partial(fused_kernel, nx, ny), out_shape=(jax.Sh...]
    unnamed x2 -> x10, local copies, waits for them, and re-layouts: 4.07 us -> 5.9 us
where the time goes in v3:
time: 68.2 us; the launch traced here: 67.9 us
  Pallas kernels  59.6 us (87%)
  local copies, waits for them, and re-layouts  5.9 us (9%)
  between operations  2.39 us (4%)
    pallas_call x1, Pallas kernels, on_device(): pl.pallas_call(functools.partial(fused_kernel, nx, ny), out_shape=(jax.Sh...  59.6 us
    unnamed x10, local copies, waits for them, and re-layouts  5.9 us

profile of v3, /device:TPU:9, one launch (start us, length us, event | category | flops | bytes accessed | tf_op | source)
XLA Modules:
  0.0 67.9 jit_solution(15330750480917656932)
XLA Ops:
  0.6 0.8 %copy.7.off_ref = s32[3,2,2]{2,1,0:T(2,128)S(1)} copy(s32[3,2,2]{0,2,1:T(2,128)} %param.8) | data formatting | bytes 96 | tf_op args[3]
  1.4 0.0 copy-start
  1.4 1.4 %copy-done = f32[3,16,32,256]{3,2,1,0:T(8,128)S(1)} copy-done((f32[3,16,32,256]{3,2,1,0:T(8,128)S(1)}, f32[3,16,32,256]{3,2,1,0:T(8,128)}, u32[]{:S(2)}) %copy-start) | copy-done | bytes 1572888
  2.8 0.0 copy-start.1
  2.8 0.9 %copy-done.1 = bf16[16,32,256]{2,1,0:T(8,128)(2,1)S(1)} copy-done((bf16[16,32,256]{2,1,0:T(8,128)(2,1)S(1)}, bf16[16,32,256]{2,1,0:T(8,128)(2,1)}, u32[]{:S(2)}) %copy-start.1) | copy-done | bytes 262168
  3.8 0.0 copy-start.2
  3.8 0.9 %copy-done.2 = bf16[16,32,256]{2,1,0:T(8,128)(2,1)S(1)} copy-done((bf16[16,32,256]{2,1,0:T(8,128)(2,1)S(1)}, bf16[16,32,256]{2,1,0:T(8,128)(2,1)}, u32[]{:S(2)}) %copy-start.2) | copy-done | bytes 262168
  4.7 0.0 copy-start.3
  4.7 0.7 copy-done.3
  5.4 59.6 %shard_map.68 = (f32[3,16,32,256]{3,2,1,0:T(8,128)S(1)}, f32[1,1]{1,0:T(1,128)}) custom-call(s32[3,2,2]{2,1,0:T(2,128)S(1)} %copy.7.off_ref, s32[2,2]{1,0:T(2,128)S(1)} %copy-done.3, bf16[16,32,256]{2,1,0:T(8,128)(2,1)S(1)} %copy-done.1, bf16[16,32,256]{2,1,0:T(8,128)(2,1)S(1)} %copy-done.2, f32[3,16,32,256]{3,2,1,0:T(8,128)S(1)} %copy-done), custom_call_target="tpu_custom_call" | custom-call | tf_op jit(solution)/shard_map/pallas_call | solution.py:580
  65.0 1.1 %copy.10 = f32[3,16,32,256]{3,2,1,0:T(8,128)} copy(f32[3,16,32,256]{3,2,1,0:T(8,128)S(1)} %get-tuple-element.8) | data formatting | bytes 3145728
Async XLA Ops:
  1.4 1.4 %copy-start = (f32[3,16,32,256]{3,2,1,0:T(8,128)S(1)}, f32[3,16,32,256]{3,2,1,0:T(8,128)}, u32[]{:S(2)}) copy-start(f32[3,16,32,256]{3,2,1,0:T(8,128)} %vel_hbm.1) | copy-start | bytes 4718596
  2.8 0.9 %copy-start.1 = (bf16[16,32,256]{2,1,0:T(8,128)(2,1)S(1)}, bf16[16,32,256]{2,1,0:T(8,128)(2,1)}, u32[]{:S(2)}) copy-start(bf16[16,32,256]{2,1,0:T(8,128)(2,1)} %mov_ref.1) | copy-start | bytes 786436
  3.8 0.9 %copy-start.2 = (bf16[16,32,256]{2,1,0:T(8,128)(2,1)S(1)}, bf16[16,32,256]{2,1,0:T(8,128)(2,1)}, u32[]{:S(2)}) copy-start(bf16[16,32,256]{2,1,0:T(8,128)(2,1)} %fix_ref.1) | copy-start | bytes 786436
  4.7 0.7 %copy-start.3 = (s32[2,2]{1,0:T(2,128)S(1)}, s32[2,2]{1,0:T(2,128)}, u32[]{:S(2)}) copy-start(s32[2,2]{1,0:T(2,128)} %tis_ref.1) | copy-start | bytes 52
